TPU v7x, 32 devices: a whole 2x2x4 slice. The times are simulated.
32 devices in a mesh: grp: 8 (over z, x), sp: 4 (over y, core).
Axes of the slice: x: 2, y: 2, z: 4, core: 2. Of those that a mesh axis runs over, the one named last changes fastest.
Arguments:
- queries: bfloat16 [8, 768, 2048], P('grp', 'sp'), may hold values from -15 to 15
- keys: bfloat16 [8, 768, 2048], P('grp', 'sp'), may hold values from -6 to 6
- values: bfloat16 [8, 768, 2048], P('grp', 'sp'), may hold values from -6 to 6
- ref_cache: bfloat16 [8, 2, 512, 2048], P('grp', None, 'sp'), may hold values from -6 to 6
- ref_ids: int32 [8], replicated, may hold values from 0 to 7
- ref_owner: int32 [8], replicated, may hold values from 0 to 7, each once
- ref_lens: int32 [8], replicated, may hold values from 64 to 512, as said below
Outputs:
- attended: bfloat16 [8, 768, 2048], P('grp', 'sp')
Inputs may be any that keep to these rules, and one draw needn't show every extreme that they name: `ref_owner`: each reference image lies in exactly one cache row. `ref_lens`: some reference has 512 live tokens and some 512 // 8.
All inputs are finite; a program needn't handle non-finite values.
Results may differ from a plain program's by a relative error of at most 0.0031.
Values may be sent and summed in bfloat16 or wider, within the bound.
A program may use at most 64 MiB of HBM per device.

v0:
```python
import math

import jax
import jax.numpy as jnp
from jax import lax
from jax.sharding import PartitionSpec as P

HEAD_DIM = 128


def attend(own_q, own_k, own_v, ref_pair, live_len):
    tokens, feat_width = own_q.shape
    head_count = feat_width // HEAD_DIM
    key_set = jnp.concatenate([own_k, ref_pair[0]], axis=0)
    value_set = jnp.concatenate([own_v, ref_pair[1]], axis=0)
    total_keys = key_set.shape[0]
    key_heads = key_set.reshape(total_keys, head_count, HEAD_DIM)
    value_heads = value_set.reshape(total_keys, head_count, HEAD_DIM)
    live_mask = jnp.arange(total_keys, dtype=jnp.int32) < tokens + live_len
    block_rows = math.gcd(tokens, 512)
    query_blocks = own_q.reshape(tokens // block_rows, block_rows, head_count, HEAD_DIM)
    score_scale = HEAD_DIM ** (-0.5)

    def one_block(query_rows):
        scores = (
            jnp.einsum("qhd,khd->hqk", query_rows, key_heads, preferred_element_type=jnp.float32)
            * score_scale
        )
        scores = jnp.where(live_mask[None, None, :], scores, -jnp.inf)
        row_peak = jnp.max(scores, axis=-1, keepdims=True)
        weights = jnp.exp(scores - row_peak)
        row_total = jnp.sum(weights, axis=-1, keepdims=True)
        soft_probs = weights.astype(jnp.bfloat16)
        mixed_out = jnp.einsum(
            "hqk,khd->qhd", soft_probs, value_heads, preferred_element_type=jnp.float32
        )
        scaled = mixed_out / jnp.transpose(row_total, (1, 0, 2))
        return scaled.astype(jnp.bfloat16).reshape(block_rows, feat_width)

    return lax.map(one_block, query_blocks).reshape(tokens, feat_width)


def row_picker(wanted, carry, piece):
    inside = jnp.logical_and(wanted >= 0, wanted < piece.shape[0])
    picked = lax.dynamic_index_in_dim(
        piece, jnp.clip(wanted, 0, piece.shape[0] - 1), 0, keepdims=False
    )
    return jnp.where(inside, picked, carry)


def shards(queries, keys, values, ref_cache, ref_ids, ref_owner, ref_lens):
    my_group = lax.axis_index("grp")
    wanted_ref = ref_ids[my_group]
    need_row = ref_owner[wanted_ref]
    need_len = ref_lens[wanted_ref]
    own_q, own_k, own_v = (
        lax.all_to_all(queries[0], "sp", split_axis=1, concat_axis=0, tiled=True),
        lax.all_to_all(keys[0], "sp", split_axis=1, concat_axis=0, tiled=True),
        lax.all_to_all(values[0], "sp", split_axis=1, concat_axis=0, tiled=True),
    )
    cache_slot = ref_cache[0]
    empty_slot = jnp.zeros_like(cache_slot)
    my_slot = row_picker(
        need_row, empty_slot, lax.all_gather(cache_slot[None], "grp", axis=0, tiled=True)
    )
    my_slot = lax.all_to_all(my_slot, "sp", split_axis=2, concat_axis=1, tiled=True)
    head_result = attend(own_q, own_k, own_v, my_slot, need_len)
    returned = lax.all_to_all(head_result, "sp", split_axis=0, concat_axis=1, tiled=True)
    return returned[None]


def solution(mesh):
    in_specs = (
        P("grp", "sp", None),
        P("grp", "sp", None),
        P("grp", "sp", None),
        P("grp", None, "sp", None),
        P(),
        P(),
        P(),
    )
    out_specs = P("grp", "sp", None)
    return jax.shard_map(shards, mesh=mesh, in_specs=in_specs, out_specs=out_specs, check_vma=False)
```

profile of v0, /device:TPU:1, one launch (start us, length us, event | category | flops | bytes accessed | tf_op | source)
XLA Modules:
  0.0 211.8 jit_solution(16920624199737168977)
XLA Ops:
  6.5 0.0 all-gather.2.cloned.1.call-start
  6.5 0.7 all-gather.2.cloned.1.call-update
  7.3 2.3 %all_to_all.62 = bf16[192,4,512]{2,1,0:T(4,128)(2,1)S(1)} reshape(bf16[1,192,2048]{2,1,0:T(8,128)(2,1)} %param.10) | data formatting | bytes 1572864 | tf_op jit(solution)/shard_map/all_to_all | solution.py:58
  9.6 1.0 copy.28
  10.6 4.3 %all-to-all-start.1 = ((bf16[192,4,512]{2,0,1:T(8,128)(2,1)}), bf16[192,4,512]{2,0,1:T(8,128)(2,1)S(1)}, u32[]{:S(2)}, u32[]{:S(2)}) async-start(bf16[192,4,512]{2,0,1:T(8,128)(2,1)} %copy.28), calls=%async_computation.1 | async-start | bytes 1572864 | tf_op jit(solution)/shard_map/all_to_all | solution.py:58
  14.9 0.0 copy-done.2
  14.9 0.6 all_to_all.68
  15.4 0.0 copy-start.3
  15.5 1.1 copy.31
  16.6 9.0 %all-to-all-done.1 = bf16[192,4,512]{2,0,1:T(8,128)(2,1)S(1)} async-done(((bf16[192,4,512]{2,0,1:T(8,128)(2,1)}), bf16[192,4,512]{2,0,1:T(8,128)(2,1)S(1)}, u32[]{:S(2)}, u32[]{:S(2)}) %all-to-all-start.1) | async-done | bytes 786464 | tf_op jit(solution)/shard_map/all_to_all | solution.py:58
  25.5 4.4 %all-to-all-start.3 = ((bf16[192,4,512]{2,0,1:T(8,128)(2,1)}), bf16[192,4,512]{2,0,1:T(8,128)(2,1)S(1)}, u32[]{:S(2)}, u32[]{:S(2)}) async-start(bf16[192,4,512]{2,0,1:T(8,128)(2,1)} %copy.31), calls=%async_computation.3 | async-start | bytes 1572864 | tf_op jit(solution)/shard_map/all_to_all | solution.py:59
  30.0 0.0 copy-done.3
  30.0 0.6 all_to_all.59
  30.6 1.0 copy.27
  31.6 9.3 %all-to-all-done.3 = bf16[192,4,512]{2,0,1:T(8,128)(2,1)S(1)} async-done(((bf16[192,4,512]{2,0,1:T(8,128)(2,1)}), bf16[192,4,512]{2,0,1:T(8,128)(2,1)S(1)}, u32[]{:S(2)}, u32[]{:S(2)}) %all-to-all-start.3) | async-done | bytes 786464 | tf_op jit(solution)/shard_map/all_to_all | solution.py:59
  40.9 4.9 %all-to-all-start = ((bf16[192,4,512]{2,0,1:T(8,128)(2,1)}), bf16[192,4,512]{2,0,1:T(8,128)(2,1)}, u32[]{:S(2)}, u32[]{:S(2)}) async-start(bf16[192,4,512]{2,0,1:T(8,128)(2,1)} %copy.27), calls=%async_computation | async-start | bytes 1572864 | tf_op jit(solution)/shard_map/all_to_all | solution.py:57
  45.8 0.0 copy-done.4
  45.8 0.7 dynamic_slice.17
  48.5 0.7 dynamic_slice.19
  51.2 84.9 %all-gather.2.cloned.1.call-done = bf16[8,2,128,2048]{3,2,1,0:T(8,128)(2,1)} async-done(((bf16[1,2,128,2048]{3,2,1,0:T(8,128)(2,1)}), bf16[8,2,128,2048]{3,2,1,0:T(8,128)(2,1)}) %all-gather.2.cloned.1.call-update) | async-done | bytes 8388624 | tf_op jit(solution)/shard_map/all_gather | solution.py:64
  136.1 1.3 select_bitcast_fusion
  137.4 0.0 copy-start.6
  137.4 2.0 copy.29
  139.4 0.0 all-to-all-done
  139.4 4.6 %all-to-all-start.2 = ((bf16[2,128,2048]{1,0,2:T(2,128)(2,1)}), bf16[2,128,2048]{1,0,2:T(2,128)(2,1)S(1)}, u32[]{:S(2)}, u32[]{:S(2)}) async-start(bf16[2,128,2048]{1,0,2:T(2,128)(2,1)} %copy.29), calls=%async_computation.2 | async-start | bytes 2097152 | tf_op jit(solution)/shard_map/all_to_all | solution.py:66
  144.0 0.0 copy-done.6
  144.0 0.6 dynamic_slice.18
  145.3 1.1 concatenate.16
  146.4 1.1 concatenate.19
  147.5 1.7 reshape.54
  149.3 8.3 %all-to-all-done.2 = bf16[2,128,2048]{1,0,2:T(2,128)(2,1)S(1)} async-done(((bf16[2,128,2048]{1,0,2:T(2,128)(2,1)}), bf16[2,128,2048]{1,0,2:T(2,128)(2,1)S(1)}, u32[]{:S(2)}, u32[]{:S(2)}) %all-to-all-start.2) | async-done | bytes 1048608 | tf_op jit(solution)/shard_map/all_to_all | solution.py:66
  157.6 0.8 copy.30
  158.4 0.9 fusion.17
  159.3 1.2 concatenate.17
  160.5 7.1 %pad_maximum_fusion = bf16[1280,4,128]{2,1,0:T(4,128)(2,1)S(1)} fusion(bf16[512,4,128]{2,1,0:T(4,128)(2,1)S(1)} %concatenate.17, bf16[768,4,128]{2,1,0:T(4,128)(2,1)S(1)} %copy-done), kind=kLoop, calls=%fused_computation.14 | loop fusion | flops 655360 | bytes 2621440 | tf_op jit(solution)/shard_map/concatenate | solution.py:14
  167.6 0.2 copy.33
  167.8 0.9 concatenate.20
  168.7 3.3 %pad_maximum_fusion.1 = bf16[1280,4,128]{2,1,0:T(4,128)(2,1)S(1)} fusion(bf16[512,4,128]{2,1,0:T(4,128)(2,1)} %concatenate.20, bf16[768,4,128]{2,1,0:T(4,128)(2,1)} %concatenate.19), kind=kLoop, calls=%fused_computation.15 | loop fusion | flops 655360 | bytes 2621440 | tf_op jit(solution)/shard_map/concatenate | solution.py:15
  172.0 2.6 %copy.34 = bf16[1280,4,128]{0,2,1:T(8,128)(2,1)} copy(bf16[1280,4,128]{2,1,0:T(4,128)(2,1)S(1)} %pad_maximum_fusion.1) | data formatting | bytes 2621440
  174.6 13.3 %while.11 = (s32[]{:T(128)}, bf16[3,256,512]{2,1,0:T(8,128)(2,1)}, bf16[3,256,4,128]{3,2,1,0:T(4,128)(2,1)S(1)}, bf16[1280,4,128]{2,0,1:T(8,128)(2,1)S(1)}, bf16...) while((s32[]{:T(128)}, bf16[3,256,512]{2,1,0:T(8,128)(2,1)}, ...), condition=%wide.region_3.4_spmd.clone, body=%wide.region_0.3_spmd.clone.sunk | while | flops 680525056 | bytes 25713776 | solution.py:40
  174.6 0.1 constant_dynamic-slice_fusion.2
  174.7 0.9 fusion.29
  175.7 1.0 fusion.30
  176.7 0.3 copy-done.1
  177.0 1.2 fusion.31
  178.2 0.1 copy.47
  178.3 0.7 constant_dynamic-update-slice_fusion.2
  179.0 0.1 constant_dynamic-slice_fusion.2
  179.1 0.9 fusion.29
  180.1 1.0 fusion.30
  181.1 0.3 copy-done.1
  181.4 1.2 fusion.31
  182.6 0.1 copy.47
  182.7 0.7 constant_dynamic-update-slice_fusion.2
  183.5 0.1 constant_dynamic-slice_fusion.2
  183.6 0.9 fusion.29
  184.5 1.0 fusion.30
  185.5 0.3 copy-done.1
  185.8 1.2 fusion.31
  187.0 0.1 copy.47
  187.2 0.7 constant_dynamic-update-slice_fusion.2
  187.9 14.9 %all_to_all.79 = bf16[4,192,512]{2,1,0:T(8,128)(2,1)S(1)} all-to-all(bf16[4,192,512]{2,1,0:T(8,128)(2,1)} %bitcast.54), channel_id=1, replica_groups=mesh['grp'=8,'sp'=4] {'sp'}, dimensions={0} | all-to-all | bytes 1572864 | tf_op jit(solution)/shard_map/all_to_all | solution.py:68
  202.8 0.6 copy.36
  203.4 1.5 broadcast_in_dim.32
  (13 shorter events, 0.0 us)
Async XLA Ops:
  6.5 8.3 %copy-start.2 = (bf16[1,192,2048]{2,1,0:T(8,128)(2,1)S(1)}, bf16[1,192,2048]{2,1,0:T(8,128)(2,1)}, u32[]{:S(2)}) copy-start(bf16[1,192,2048]{2,1,0:T(8,128)(2,1)} %param.11) | copy-start | bytes 2359300
  6.5 129.6 %all-gather.2.cloned.1.call-start = ((), (), s32[]{:S(2)}) async-start(), calls=%async_computation.5 | async-start | bytes 9437184 | tf_op jit(solution)/shard_map/all_gather | solution.py:64
  10.6 15.0 %all-to-all-start.1 = ((bf16[192,4,512]{2,0,1:T(8,128)(2,1)}), bf16[192,4,512]{2,0,1:T(8,128)(2,1)S(1)}, u32[]{:S(2)}, u32[]{:S(2)}) async-start(bf16[192,4,512]{2,0,1:T(8,128)(2,1)} %copy.28), calls=%async_computation.1 | async-start | bytes 1572864 | tf_op jit(solution)/shard_map/all_to_all | solution.py:58
  15.4 14.5 %copy-start.3 = (bf16[1,192,2048]{2,1,0:T(8,128)(2,1)S(1)}, bf16[1,192,2048]{2,1,0:T(8,128)(2,1)}, u32[]{:S(2)}) copy-start(bf16[1,192,2048]{2,1,0:T(8,128)(2,1)} %param.9) | copy-start | bytes 2359300
  25.5 15.3 %all-to-all-start.3 = ((bf16[192,4,512]{2,0,1:T(8,128)(2,1)}), bf16[192,4,512]{2,0,1:T(8,128)(2,1)S(1)}, u32[]{:S(2)}, u32[]{:S(2)}) async-start(bf16[192,4,512]{2,0,1:T(8,128)(2,1)} %copy.31), calls=%async_computation.3 | async-start | bytes 1572864 | tf_op jit(solution)/shard_map/all_to_all | solution.py:59
  30.0 15.8 %copy-start.4 = (s32[8]{0:T(128)S(1)}, s32[8]{0:T(128)}, u32[]{:S(2)}) copy-start(s32[8]{0:T(128)} %param.13) | copy-start | bytes 100
  30.0 18.5 %copy-start.5 = (s32[8]{0:T(128)S(1)}, s32[8]{0:T(128)}, u32[]{:S(2)}) copy-start(s32[8]{0:T(128)} %param.14) | copy-start | bytes 100
  40.9 98.6 %all-to-all-start = ((bf16[192,4,512]{2,0,1:T(8,128)(2,1)}), bf16[192,4,512]{2,0,1:T(8,128)(2,1)}, u32[]{:S(2)}, u32[]{:S(2)}) async-start(bf16[192,4,512]{2,0,1:T(8,128)(2,1)} %copy.27), calls=%async_computation | async-start | bytes 1572864 | tf_op jit(solution)/shard_map/all_to_all | solution.py:57
  137.4 6.6 %copy-start.6 = (s32[8]{0:T(128)S(1)}, s32[8]{0:T(128)}, u32[]{:S(2)}) copy-start(s32[8]{0:T(128)} %param.15) | copy-start | bytes 100
  139.4 18.2 %all-to-all-start.2 = ((bf16[2,128,2048]{1,0,2:T(2,128)(2,1)}), bf16[2,128,2048]{1,0,2:T(2,128)(2,1)S(1)}, u32[]{:S(2)}, u32[]{:S(2)}) async-start(bf16[2,128,2048]{1,0,2:T(2,128)(2,1)} %copy.29), calls=%async_computation.2 | async-start | bytes 2097152 | tf_op jit(solution)/shard_map/all_to_all | solution.py:66
  158.4 2.1 copy-start
  175.6 1.3 copy-start.1
  180.1 1.3 copy-start.1
  184.5 1.3 copy-start.1
Sparse Core Ops, SparseCore 0:
  9.5 126.5 all-gather.1
where the time goes:
time: 213 us; the launch traced here: 212 us
  waiting for transfers between devices  112 us (53%)
  local copies, waits for them, and re-layouts  26.9 us (13%)
  between operations  18.3 us (9%)
  starting transfers between devices  18.2 us (9%)
  blocking collectives  14.9 us (7%)
  other arithmetic  14.8 us (7%)
  matrix products  6.34 us (3%)
    all_gather x1, waiting for transfers between devices, shards(): lax.all_gather(cache_slot[None], 'grp', axis=0, tiled=True)  84.9 us
    all_to_all x1, blocking collectives, shards(): lax.all_to_all(head_result, 'sp', split_axis=0, concat_axis=1, tiled=True)  14.9 us
    all_to_all x1, waiting for transfers between devices, shards(): lax.all_to_all(values[0], 'sp', split_axis=1, concat_axis=0, tiled=True)  9.29 us
    all_to_all x1, waiting for transfers between devices, shards(): lax.all_to_all(keys[0], 'sp', split_axis=1, concat_axis=0, tiled=True)  8.98 us
    all_to_all x1, waiting for transfers between devices, shards(): lax.all_to_all(my_slot, 'sp', split_axis=2, concat_axis=1, tiled=True)  8.31 us
    concatenate x1, other arithmetic, attend(): key_set = jnp.concatenate([own_k, ref_pair[0]], axis=0)  7.1 us
    all_to_all x1, starting transfers between devices, shards(): lax.all_to_all(queries[0], 'sp', split_axis=1, concat_axis=0, tiled=True)  4.93 us
    all_to_all x1, starting transfers between devices, shards(): lax.all_to_all(my_slot, 'sp', split_axis=2, concat_axis=1, tiled=True)  4.56 us
  transfers between devices with their start and end apart: 5, of which 4 were waited for; matrix products, arithmetic and copies ran while one was open for 6% of the time, Pallas kernels for 0%

commit v1 on v0

v1 whole, which is shorter than its diff:
```python
import functools

import jax
import jax.numpy as jnp
from jax import lax
from jax.experimental import pallas as pl
from jax.experimental.pallas import tpu as pltpu
from jax.sharding import PartitionSpec as P

HEAD_DIM = 128
PAIR = 2
MESH = pl.DeviceIdType.MESH


def slots_on(p, levels):
    return min(PAIR * (p + 1), levels - 1 - p)


def sends_rows(p, levels):
    return PAIR * (p + 1) <= levels - 1 - p


def pick(options):
    value = options[-1][1]
    for cond, other in reversed(options[:-1]):
        value = lax.select(cond, other, value)
    return value


def kernel(
    n_grp, n_sp,
    ids_ref, owner_ref, lens_ref, q_hbm, k_hbm, v_hbm, ref_hbm, out_hbm,
    q_buf, k_buf, v_buf, own_buf, x_buf, line_in, line_out, routed, ref_kv, o_buf,
    own_sem, keep_sem, seq_send, seq_recv, x_send, x_recv, line_send, line_recv,
    ref_send, ref_recv, o_keep, o_send, o_recv,
):
    levels = n_grp // PAIR
    heads = ref_hbm.shape[-1] // HEAD_DIM
    per_dev = heads // n_sp
    feat = per_dev * HEAD_DIM
    tokens = q_hbm.shape[1]
    ref_tokens = ref_hbm.shape[2]
    grp = lax.axis_index("grp")
    sp = lax.axis_index("sp")
    level = grp // PAIR
    side = grp % PAIR
    mate = level * PAIR + (1 - side)

    def at_level(other):
        return (other * PAIR + side, sp)

    barrier = pltpu.get_barrier_semaphore()

    def greet(device):
        pl.semaphore_signal(barrier, inc=1, device_id=device, device_id_type=MESH)

    greet((mate, sp))
    for step in range(1, n_sp):
        greet((grp, (sp + step) % n_sp))

    @pl.when(level > 0)
    def _():
        greet(at_level(level - 1))

    @pl.when(level < levels - 1)
    def _():
        greet(at_level(level + 1))

    inner = jnp.logical_and(level > 0, level < levels - 1)
    pl.semaphore_wait(barrier, n_sp + 1 + inner.astype(jnp.int32))

    def head_of(c):
        return (c + sp) % n_sp, c // n_sp

    def lanes_of(c):
        dest, local = head_of(c)
        return pl.ds(pl.multiple_of((dest * per_dev + local) * HEAD_DIM, HEAD_DIM), HEAD_DIM)

    def own_copy(c):
        return pltpu.make_async_copy(
            ref_hbm.at[0, :, :, lanes_of(c)], own_buf.at[c], own_sem.at[c]
        )

    def x_copy(c):
        return pltpu.make_async_remote_copy(
            src_ref=ref_hbm.at[0, :, :, lanes_of(c)], dst_ref=x_buf.at[c],
            send_sem=x_send.at[c], recv_sem=x_recv.at[c],
            device_id=(mate, sp), device_id_type=MESH,
        )

    def line_copy(way, slot, c, src, other):
        return pltpu.make_async_remote_copy(
            src_ref=src, dst_ref=line_in.at[way, slot, c],
            send_sem=line_send.at[way, slot, c], recv_sem=line_recv.at[way, slot, c],
            device_id=at_level(other), device_id_type=MESH,
        )

    def ref_copy(c, dest, local, src):
        return pltpu.make_async_remote_copy(
            src_ref=routed.at[c], dst_ref=ref_kv.at[local, src],
            send_sem=ref_send.at[c], recv_sem=ref_recv.at[local, src],
            device_id=(grp, dest), device_id_type=MESH,
        )

    seq_pairs = ((q_hbm, q_buf), (k_hbm, k_buf), (v_hbm, v_buf))

    def seq_lanes(dest):
        return pl.ds(pl.multiple_of(dest * feat, HEAD_DIM), feat)

    def seq_copy(a, dest, src):
        hbm, buf = seq_pairs[a]
        return pltpu.make_async_remote_copy(
            src_ref=hbm.at[0, :, seq_lanes(dest)], dst_ref=buf.at[src],
            send_sem=seq_send.at[a, dest], recv_sem=seq_recv.at[a, src],
            device_id=(grp, dest), device_id_type=MESH,
        )

    def keep_copy(a):
        hbm, buf = seq_pairs[a]
        return pltpu.make_async_copy(
            hbm.at[0, :, seq_lanes(sp)], buf.at[sp], keep_sem.at[a]
        )

    def o_copy(local, dest, src):
        lanes = pl.ds(pl.multiple_of(local * HEAD_DIM, HEAD_DIM), HEAD_DIM)
        out_lanes = pl.ds(pl.multiple_of(src * feat + local * HEAD_DIM, HEAD_DIM), HEAD_DIM)
        return pltpu.make_async_remote_copy(
            src_ref=o_buf.at[dest, :, lanes], dst_ref=out_hbm.at[0, :, out_lanes],
            send_sem=o_send.at[local, dest], recv_sem=o_recv.at[local, src],
            device_id=(grp, dest), device_id_type=MESH,
        )

    def o_here(local):
        lanes = pl.ds(pl.multiple_of(local * HEAD_DIM, HEAD_DIM), HEAD_DIM)
        out_lanes = pl.ds(pl.multiple_of(sp * feat + local * HEAD_DIM, HEAD_DIM), HEAD_DIM)
        return pltpu.make_async_copy(
            o_buf.at[sp, :, lanes], out_hbm.at[0, :, out_lanes], o_keep.at[local]
        )

    def loop(count, body):
        def step(i, carry):
            body(i)
            return carry
        lax.fori_loop(0, count, step, 0)

    @functools.partial(loop, heads)
    def _(c):
        x_copy(c).start()
        own_copy(c).start()

    @functools.partial(loop, n_sp - 1)
    def _(step):
        dest = (sp + 1 + step) % n_sp
        for a in range(3):
            seq_copy(a, dest, sp).start()

    for a in range(3):
        keep_copy(a).start()

    @functools.partial(loop, heads)
    def _(c):
        own_copy(c).wait()

    wanted = [owner_ref[ids_ref[lev * PAIR + side]] for lev in range(levels)]
    here = ids_ref[grp]
    my_row = owner_ref[here]
    live = lens_ref[here]

    def level_rows(c):
        own, other = own_buf[c], x_buf[c]
        return [lax.select(side == k, own, other) for k in range(PAIR)]

    for at, way in ((0, 0), (levels - 1, 1)):
        @pl.when(level == at)
        def _(at=at, way=way):
            ahead = at + 1 if way == 0 else at - 1

            @functools.partial(loop, heads)
            def _(c):
                line_copy(way, side, c, own_buf.at[c], ahead).start()
                x_copy(c).wait_recv()
                line_copy(way, 1 - side, c, x_buf.at[c], ahead).start()

    def place(way, lev):
        return lev if way == 0 else levels - 1 - lev

    def relay(at, way, c):
        p = place(way, at)
        ahead = at + 1 if way == 0 else at - 1
        for slot in range(slots_on(p - 1, levels)):
            line_copy(way, slot, c, x_buf.at[c], at).wait_recv()
        if p == levels - 1:
            return
        count = slots_on(p, levels)
        if sends_rows(p, levels):
            for slot in range(PAIR * p):
                line_copy(way, slot, c, line_in.at[way, slot, c], ahead).start()
            line_copy(way, PAIR * p + side, c, own_buf.at[c], ahead).start()
            line_copy(way, PAIR * p + 1 - side, c, x_buf.at[c], ahead).start()
            return
        rows = level_rows(c)
        for slot in range(count):
            row = wanted[place(way, p + 1 + slot)]
            value = pick(line_options(at, way, c, row, slot + 1, rows))
            line_out[way, slot, c] = value
            line_copy(way, slot, c, line_out.at[way, slot, c], ahead).start()

    def line_options(at, way, c, row, slot, rows):
        p = place(way, at)
        options = [(row == at * PAIR + k, rows[k]) for k in range(PAIR)]
        if p == 0:
            return options
        if sends_rows(p - 1, levels):
            return options + [
                (row == place(way, q) * PAIR + k, line_in[way, PAIR * q + k, c])
                for q in range(p) for k in range(PAIR)
            ]
        return options + [(row // PAIR < at if way == 0 else row // PAIR > at, line_in[way, slot, c])]

    def final(at, c):
        rows = level_rows(c)
        options = line_options(at, 0, c, my_row, 0, rows)
        options = options + line_options(at, 1, c, my_row, 0, rows)[PAIR:]
        value = pick(options)
        dest, local = head_of(c)

        @pl.when(dest == sp)
        def _():
            ref_kv[local, sp] = value

        @pl.when(dest != sp)
        def _():
            routed[c] = value
            ref_copy(c, dest, local, sp).start()

    def attend(local, block):
        lanes = pl.ds(pl.multiple_of(local * HEAD_DIM, HEAD_DIM), HEAD_DIM)
        own_keys, ref_keys = n_sp * tokens, n_sp * ref_tokens
        q = q_buf[block, :, lanes]
        k = k_buf[:, :, lanes].reshape(own_keys, HEAD_DIM)
        v = v_buf[:, :, lanes].reshape(own_keys, HEAD_DIM)
        ref_k = ref_kv[local, :, 0].reshape(ref_keys, HEAD_DIM)
        ref_v = ref_kv[local, :, 1].reshape(ref_keys, HEAD_DIM)
        contract = (((1,), (1,)), ((), ()))
        scale = HEAD_DIM ** -0.5
        s_own = lax.dot_general(q, k, contract, preferred_element_type=jnp.float32) * scale
        s_ref = lax.dot_general(q, ref_k, contract, preferred_element_type=jnp.float32) * scale
        col = lax.broadcasted_iota(jnp.int32, s_ref.shape, 1)
        s_ref = jnp.where(col < live, s_ref, -jnp.inf)
        peak = jnp.maximum(
            jnp.max(s_own, axis=1, keepdims=True), jnp.max(s_ref, axis=1, keepdims=True)
        )
        w_own = jnp.exp(s_own - peak)
        w_ref = jnp.exp(s_ref - peak)
        total = jnp.sum(w_own, axis=1, keepdims=True) + jnp.sum(w_ref, axis=1, keepdims=True)
        mixed = jnp.dot(w_own.astype(jnp.bfloat16), v, preferred_element_type=jnp.float32)
        mixed += jnp.dot(w_ref.astype(jnp.bfloat16), ref_v, preferred_element_type=jnp.float32)
        o_buf[block, :, lanes] = (mixed / total).astype(jnp.bfloat16)

    last_lag = levels - 2
    first_unit = max(n_sp - 1 + last_lag, 3 * heads // 4)
    units = per_dev * n_sp

    @functools.partial(loop, max(heads + last_lag, first_unit + units))
    def _(i):
        @pl.when(jnp.logical_and(inner, i < heads))
        def _():
            x_copy(i).wait_recv()

        for at in range(levels):
            @pl.when(level == at)
            def _(at=at):
                for way in (0, 1):
                    p = place(way, at)
                    if p == 0:
                        continue
                    c = i - (p - 1)

                    @pl.when(jnp.logical_and(c >= 0, c < heads))
                    def _(c=c, way=way):
                        relay(at, way, c)

                done = i - last_lag

                @pl.when(jnp.logical_and(done >= 0, done < heads))
                def _():
                    final(at, done)

        unit = i - first_unit

        @pl.when(jnp.logical_and(unit >= 0, unit < units))
        def _():
            local, turn = unit // n_sp, unit % n_sp
            block = (sp + 1 + turn) % n_sp

            @pl.when(unit == 0)
            def _():
                for a in range(3):
                    keep_copy(a).wait()

                @functools.partial(loop, n_sp - 1)
                def _(step):
                    src = (sp + 1 + step) % n_sp
                    for a in range(3):
                        seq_copy(a, sp, src).wait_recv()

            @pl.when(turn == 0)
            def _():
                @functools.partial(loop, n_sp - 1)
                def _(step):
                    src = (sp + 1 + step) % n_sp
                    ref_copy(0, sp, local, src).wait_recv()

            attend(local, block)

            @pl.when(block == sp)
            def _():
                o_here(local).start()

            @pl.when(block != sp)
            def _():
                o_copy(local, block, sp).start()

    @functools.partial(loop, heads)
    def _(c):
        x_copy(c).wait_send()
        dest, local = head_of(c)

        @pl.when(dest != sp)
        def _():
            ref_copy(c, dest, local, sp).wait_send()

        for at in range(levels):
            @pl.when(level == at)
            def _(at=at):
                for way in (0, 1):
                    p = place(way, at)
                    if p < levels - 1:
                        for slot in range(slots_on(p, levels)):
                            line_copy(way, slot, c, x_buf.at[c], at).wait_send()

    @functools.partial(loop, n_sp - 1)
    def _(step):
        other = (sp + 1 + step) % n_sp
        for a in range(3):
            seq_copy(a, other, sp).wait_send()
        for local in range(per_dev):
            o_copy(local, other, sp).wait_send()
            o_copy(local, sp, other).wait_recv()

    for local in range(per_dev):
        o_here(local).wait()


def shards(n_grp, n_sp, queries, keys, values, ref_cache, ref_ids, ref_owner, ref_lens):
    tokens, width = queries.shape[1:]
    ref_tokens = ref_cache.shape[2]
    heads = width // HEAD_DIM
    per_dev = heads // n_sp
    feat = per_dev * HEAD_DIM
    levels = n_grp // PAIR
    slots = max(slots_on(p, levels) for p in range(levels - 1))
    chunk = (2, ref_tokens, HEAD_DIM)
    bf16 = jnp.bfloat16
    dma = pltpu.SemaphoreType.DMA
    smem = pl.BlockSpec(memory_space=pltpu.SMEM)
    hbm = pl.BlockSpec(memory_space=pl.ANY)
    all_keys = n_sp * (tokens + ref_tokens)
    return pl.pallas_call(
        functools.partial(kernel, n_grp, n_sp),
        out_shape=jax.ShapeDtypeStruct(queries.shape, bf16),
        in_specs=[smem] * 3 + [hbm] * 4,
        out_specs=hbm,
        scratch_shapes=[
            pltpu.VMEM((n_sp, tokens, feat), bf16),
            pltpu.VMEM((n_sp, tokens, feat), bf16),
            pltpu.VMEM((n_sp, tokens, feat), bf16),
            pltpu.VMEM((heads,) + chunk, bf16),
            pltpu.VMEM((heads,) + chunk, bf16),
            pltpu.VMEM((2, slots, heads) + chunk, bf16),
            pltpu.VMEM((2, slots, heads) + chunk, bf16),
            pltpu.VMEM((heads,) + chunk, bf16),
            pltpu.VMEM((per_dev, n_sp) + chunk, bf16),
            pltpu.VMEM((n_sp, tokens, feat), bf16),
            dma((heads,)),
            dma((3,)),
            dma((3, n_sp)),
            dma((3, n_sp)),
            dma((heads,)),
            dma((heads,)),
            dma((2, slots, heads)),
            dma((2, slots, heads)),
            dma((heads,)),
            dma((per_dev, n_sp)),
            dma((per_dev,)),
            dma((per_dev, n_sp)),
            dma((per_dev, n_sp)),
        ],
        compiler_params=pltpu.CompilerParams(
            collective_id=0, has_side_effects=True, vmem_limit_bytes=60 * 1024 * 1024
        ),
        cost_estimate=pl.CostEstimate(
            flops=4 * n_sp * tokens * all_keys * feat,
            bytes_accessed=8 * tokens * width * 2,
            transcendentals=per_dev * n_sp * tokens * all_keys,
        ),
    )(ref_ids, ref_owner, ref_lens, queries, keys, values, ref_cache)


def solution(mesh):
    in_specs = (
        P("grp", "sp", None),
        P("grp", "sp", None),
        P("grp", "sp", None),
        P("grp", None, "sp", None),
        P(),
        P(),
        P(),
    )
    body = functools.partial(shards, mesh.shape["grp"], mesh.shape["sp"])
    return jax.shard_map(
        body, mesh=mesh, in_specs=in_specs, out_specs=P("grp", "sp", None), check_vma=False
    )
```

time: 213 us -> 86.5 us (0.41)
  waiting for transfers between devices: 112 us -> 0 us
  Pallas kernels: 0 us -> 84.2 us
  local copies, waits for them, and re-layouts: 26.9 us -> 2.09 us
  between operations: 18.3 us -> 0.01 us
  starting transfers between devices: 18.2 us -> 0 us
  blocking collectives: 14.9 us -> 0 us
  other arithmetic: 14.8 us -> 0 us
  matrix products: 6.34 us -> 0 us
    all_gather x1 -> x0, waiting for transfers between devices: 84.9 us -> none  [shards(): lax.all_gather(cache_slot[None], 'grp', axis=0, tiled=True)]
    pallas_call x0 -> x1, Pallas kernels: none -> 84.2 us  [shards(): pl.pallas_call(functools.partial(kernel, n_grp, n_sp), out_shape=jax.Shap...]
    all_to_all x4 -> x0, waiting for transfers between devices: 26.6 us -> none  [the longest x1 9.29 us: shards(): lax.all_to_all(values[0], 'sp', split_axis=1, concat_axis=0, tiled=True)]
    all_to_all x4 -> x0, starting transfers between devices: 18.2 us -> none  [the longest x1 4.93 us: shards(): lax.all_to_all(queries[0], 'sp', split_axis=1, concat_axis=0, tiled=True)]
    all_to_all x1 -> x0, blocking collectives: 14.9 us -> none  [shards(): lax.all_to_all(head_result, 'sp', split_axis=0, concat_axis=1, tiled=True)]
    concatenate x2 -> x0, other arithmetic: 10.4 us -> none  [the longest x1 7.1 us: attend(): key_set = jnp.concatenate([own_k, ref_pair[0]], axis=0)]
    all_to_all x8 -> x0, local copies, waits for them, and re-layouts: 7.99 us -> none  [the longest x2 3.31 us: shards(): lax.all_to_all(keys[0], 'sp', split_axis=1, concat_axis=0, tiled=True)]
    dot_general x6 -> x0, matrix products: 6.34 us -> none  [the longest x3 3.51 us: one_block(): jnp.einsum('hqk,khd->qhd', soft_probs, value_heads, preferred_element_typ...]
  transfers between devices with their start and end apart: 5 -> 0, of which waited for: 4 -> 0; matrix products, arithmetic and copies ran while one was open for 6% -> 0% of each run, Pallas kernels for 0% -> 0%
where the time goes in v1:
time: 86.5 us; the launch traced here: 86.3 us
  Pallas kernels  84.2 us (97%)
  local copies, waits for them, and re-layouts  2.09 us (2%)
    pallas_call x1, Pallas kernels, shards(): pl.pallas_call(functools.partial(kernel, n_grp, n_sp), out_shape=jax.Shap...  84.2 us
    unnamed x1, local copies, waits for them, and re-layouts  2.09 us

profile of v1, /device:TPU:1, one launch (start us, length us, event | category | flops | bytes accessed | tf_op | source)
XLA Modules:
  0.0 86.3 jit_solution(1986332809581402327)
XLA Ops:
  0.0 84.2 %shard_map.73 = bf16[1,192,2048]{2,1,0:T(8,128)(2,1)} custom-call(s32[8]{0:T(128)} %ids_ref.1, s32[8]{0:T(128)} %owner_ref.1, s32[8]{0:T(128)} %lens_ref.1, bf16[1,192,2048]{2,1,0:T(8,128)(2,1)} %q_hbm.1, bf16[1,192,2048]{2,1,0:T(8,128)(2,1)} %k_hbm.1, bf16[1,192,2048]{2,1,0:T(8,128)(2,1)} %v_hbm.1, bf16[1,2,128,2048]{3,2,1,0:T(8,128)(2,1)} %ref_hbm.1), custom_call_target="tpu_custom_call" | custom-call | flops 2013265920 | bytes 6291456 | tf_op jit(solution)/shard_map/pallas_call | solution.py:369
  84.2 2.1 %copy.9 = bf16[1,192,2048]{2,1,0:T(8,128)(2,1)} copy(bf16[1,192,2048]{2,1,0:T(8,128)(2,1)} %shard_map.73) | data formatting | bytes 1572864

commit v2 on v1

--- a/solution.py
+++ b/solution.py
@@ -143,16 +143,17 @@
             return carry
         lax.fori_loop(0, count, step, 0)
 
+    x_ahead, ends_ahead = 5, 3
+    seq_copies = 3 * (n_sp - 1)
+    per_step = -(-seq_copies // 9)
+
+    @functools.partial(loop, x_ahead)
+    def _(c):
+        x_copy(c).start()
+
     @functools.partial(loop, heads)
     def _(c):
-        x_copy(c).start()
         own_copy(c).start()
-
-    @functools.partial(loop, n_sp - 1)
-    def _(step):
-        dest = (sp + 1 + step) % n_sp
-        for a in range(3):
-            seq_copy(a, dest, sp).start()
 
     for a in range(3):
         keep_copy(a).start()
@@ -170,16 +171,18 @@
         own, other = own_buf[c], x_buf[c]
         return [lax.select(side == k, own, other) for k in range(PAIR)]
 
-    for at, way in ((0, 0), (levels - 1, 1)):
+    def send_rows(at, c):
+        way, ahead = (0, at + 1) if at == 0 else (1, at - 1)
+        line_copy(way, side, c, own_buf.at[c], ahead).start()
+        x_copy(c).wait_recv()
+        line_copy(way, 1 - side, c, x_buf.at[c], ahead).start()
+
+    for at in (0, levels - 1):
         @pl.when(level == at)
-        def _(at=at, way=way):
-            ahead = at + 1 if way == 0 else at - 1
-
-            @functools.partial(loop, heads)
+        def _(at=at):
+            @functools.partial(loop, ends_ahead)
             def _(c):
-                line_copy(way, side, c, own_buf.at[c], ahead).start()
-                x_copy(c).wait_recv()
-                line_copy(way, 1 - side, c, x_buf.at[c], ahead).start()
+                send_rows(at, c)
 
     def place(way, lev):
         return lev if way == 0 else levels - 1 - lev
@@ -255,14 +258,19 @@
         total = jnp.sum(w_own, axis=1, keepdims=True) + jnp.sum(w_ref, axis=1, keepdims=True)
         mixed = jnp.dot(w_own.astype(jnp.bfloat16), v, preferred_element_type=jnp.float32)
         mixed += jnp.dot(w_ref.astype(jnp.bfloat16), ref_v, preferred_element_type=jnp.float32)
-        o_buf[block, :, lanes] = (mixed / total).astype(jnp.bfloat16)
+        return (mixed / total).astype(jnp.bfloat16)
 
     last_lag = levels - 2
-    first_unit = max(n_sp - 1 + last_lag, 3 * heads // 4)
     units = per_dev * n_sp
-
-    @functools.partial(loop, max(heads + last_lag, first_unit + units))
+    at_once = 2
+    first_unit = heads - 1 + last_lag - (per_dev - 1) * n_sp // at_once
+
+    @functools.partial(loop, max(heads + last_lag, first_unit + units // at_once))
     def _(i):
+        @pl.when(i + x_ahead < heads)
+        def _():
+            x_copy(i + x_ahead).start()
+
         @pl.when(jnp.logical_and(inner, i < heads))
         def _():
             x_copy(i).wait_recv()
@@ -270,6 +278,11 @@
         for at in range(levels):
             @pl.when(level == at)
             def _(at=at):
+                if at in (0, levels - 1):
+                    @pl.when(i + ends_ahead < heads)
+                    def _():
+                        send_rows(at, i + ends_ahead)
+
                 for way in (0, 1):
                     p = place(way, at)
                     if p == 0:
@@ -286,12 +299,22 @@
                 def _():
                     final(at, done)
 
-        unit = i - first_unit
+        for n in range(per_step):
+            number = i * per_step + n
+
+            @pl.when(number < seq_copies)
+            def _(number=number):
+                dest = (sp + 1 + number // 3) % n_sp
+                for a in range(3):
+                    @pl.when(number % 3 == a)
+                    def _(a=a):
+                        seq_copy(a, dest, sp).start()
+
+        unit = (i - first_unit) * at_once
 
         @pl.when(jnp.logical_and(unit >= 0, unit < units))
         def _():
             local, turn = unit // n_sp, unit % n_sp
-            block = (sp + 1 + turn) % n_sp
 
             @pl.when(unit == 0)
             def _():
@@ -311,15 +334,19 @@
                     src = (sp + 1 + step) % n_sp
                     ref_copy(0, sp, local, src).wait_recv()
 
-            attend(local, block)
-
-            @pl.when(block == sp)
-            def _():
-                o_here(local).start()
-
-            @pl.when(block != sp)
-            def _():
-                o_copy(local, block, sp).start()
+            lanes = pl.ds(pl.multiple_of(local * HEAD_DIM, HEAD_DIM), HEAD_DIM)
+            blocks = [(sp + 1 + turn + n) % n_sp for n in range(at_once)]
+            results = [attend(local, block) for block in blocks]
+            for block, result in zip(blocks, results):
+                o_buf[block, :, lanes] = result
+            for block in blocks:
+                @pl.when(block == sp)
+                def _():
+                    o_here(local).start()
+
+                @pl.when(block != sp)
+                def _(block=block):
+                    o_copy(local, block, sp).start()
 
     @functools.partial(loop, heads)
     def _(c):

time: 86.5 us -> 82.5 us (0.954)
  Pallas kernels: 84.2 us -> 79.9 us
    pallas_call x1, Pallas kernels: 84.2 us -> 79.9 us  [shards(): pl.pallas_call(functools.partial(kernel, n_grp, n_sp), out_shape=jax.Shap...]
where the time goes in v2:
time: 82.5 us; the launch traced here: 82 us
  Pallas kernels  79.9 us (97%)
  local copies, waits for them, and re-layouts  2.09 us (3%)
    pallas_call x1, Pallas kernels, shards(): pl.pallas_call(functools.partial(kernel, n_grp, n_sp), out_shape=jax.Shap...  79.9 us
    unnamed x1, local copies, waits for them, and re-layouts  2.09 us

profile of v2, /device:TPU:1, one launch (start us, length us, event | category | flops | bytes accessed | tf_op | source)
XLA Modules:
  0.0 82.0 jit_solution(1755319016258751535)
XLA Ops:
  0.0 79.9 %shard_map.73 = bf16[1,192,2048]{2,1,0:T(8,128)(2,1)} custom-call(s32[8]{0:T(128)} %ids_ref.1, s32[8]{0:T(128)} %owner_ref.1, s32[8]{0:T(128)} %lens_ref.1, bf16[1,192,2048]{2,1,0:T(8,128)(2,1)} %q_hbm.1, bf16[1,192,2048]{2,1,0:T(8,128)(2,1)} %k_hbm.1, bf16[1,192,2048]{2,1,0:T(8,128)(2,1)} %v_hbm.1, bf16[1,2,128,2048]{3,2,1,0:T(8,128)(2,1)} %ref_hbm.1), custom_call_target="tpu_custom_call" | custom-call | flops 2013265920 | bytes 6291456 | tf_op jit(solution)/shard_map/pallas_call | solution.py:396
  79.9 2.1 %copy.9 = bf16[1,192,2048]{2,1,0:T(8,128)(2,1)} copy(bf16[1,192,2048]{2,1,0:T(8,128)(2,1)} %shard_map.73) | data formatting | bytes 1572864

commit v3 on v2

--- a/solution.py
+++ b/solution.py
@@ -143,7 +143,7 @@
             return carry
         lax.fori_loop(0, count, step, 0)
 
-    x_ahead, ends_ahead = 5, 3
+    x_ahead, ends_ahead = 8, 6
     seq_copies = 3 * (n_sp - 1)
     per_step = -(-seq_copies // 9)
 
@@ -260,7 +260,7 @@
         mixed += jnp.dot(w_ref.astype(jnp.bfloat16), ref_v, preferred_element_type=jnp.float32)
         return (mixed / total).astype(jnp.bfloat16)
 
-    last_lag = levels - 2
+    last_lag = levels - 1
     units = per_dev * n_sp
     at_once = 2
     first_unit = heads - 1 + last_lag - (per_dev - 1) * n_sp // at_once
@@ -283,11 +283,10 @@
                     def _():
                         send_rows(at, i + ends_ahead)
 
-                for way in (0, 1):
-                    p = place(way, at)
+                for p, way in sorted((place(way, at), way) for way in (0, 1)):
                     if p == 0:
                         continue
-                    c = i - (p - 1)
+                    c = i - (0 if p == 1 else p)
 
                     @pl.when(jnp.logical_and(c >= 0, c < heads))
                     def _(c=c, way=way):

time: 82.5 us -> 74.8 us (0.907)
  Pallas kernels: 79.9 us -> 72.5 us
    pallas_call x1, Pallas kernels: 79.9 us -> 72.5 us  [shards(): pl.pallas_call(functools.partial(kernel, n_grp, n_sp), out_shape=jax.Shap...]
where the time goes in v3:
time: 74.8 us; the launch traced here: 74.6 us
  Pallas kernels  72.5 us (97%)
  local copies, waits for them, and re-layouts  2.09 us (3%)
    pallas_call x1, Pallas kernels, shards(): pl.pallas_call(functools.partial(kernel, n_grp, n_sp), out_shape=jax.Shap...  72.5 us
    unnamed x1, local copies, waits for them, and re-layouts  2.09 us

profile of v3, /device:TPU:1, one launch (start us, length us, event | category | flops | bytes accessed | tf_op | source)
XLA Modules:
  0.0 74.6 jit_solution(10048867481077042003)
XLA Ops:
  0.0 72.5 %shard_map.73 = bf16[1,192,2048]{2,1,0:T(8,128)(2,1)} custom-call(s32[8]{0:T(128)} %ids_ref.1, s32[8]{0:T(128)} %owner_ref.1, s32[8]{0:T(128)} %lens_ref.1, bf16[1,192,2048]{2,1,0:T(8,128)(2,1)} %q_hbm.1, bf16[1,192,2048]{2,1,0:T(8,128)(2,1)} %k_hbm.1, bf16[1,192,2048]{2,1,0:T(8,128)(2,1)} %v_hbm.1, bf16[1,2,128,2048]{3,2,1,0:T(8,128)(2,1)} %ref_hbm.1), custom_call_target="tpu_custom_call" | custom-call | flops 2013265920 | bytes 6291456 | tf_op jit(solution)/shard_map/pallas_call | solution.py:395
  72.5 2.1 %copy.9 = bf16[1,192,2048]{2,1,0:T(8,128)(2,1)} copy(bf16[1,192,2048]{2,1,0:T(8,128)(2,1)} %shard_map.73) | data formatting | bytes 1572864

commit v4 on v3

--- a/solution.py
+++ b/solution.py
@@ -143,24 +143,13 @@
             return carry
         lax.fori_loop(0, count, step, 0)
 
-    x_ahead, ends_ahead = 8, 6
+    x_ahead, ends_ahead = 10, 8
     seq_copies = 3 * (n_sp - 1)
     per_step = -(-seq_copies // 9)
 
     @functools.partial(loop, x_ahead)
     def _(c):
         x_copy(c).start()
-
-    @functools.partial(loop, heads)
-    def _(c):
-        own_copy(c).start()
-
-    for a in range(3):
-        keep_copy(a).start()
-
-    @functools.partial(loop, heads)
-    def _(c):
-        own_copy(c).wait()
 
     wanted = [owner_ref[ids_ref[lev * PAIR + side]] for lev in range(levels)]
     here = ids_ref[grp]
@@ -171,9 +160,13 @@
         own, other = own_buf[c], x_buf[c]
         return [lax.select(side == k, own, other) for k in range(PAIR)]
 
-    def send_rows(at, c):
+    def send_own(at, c):
         way, ahead = (0, at + 1) if at == 0 else (1, at - 1)
-        line_copy(way, side, c, own_buf.at[c], ahead).start()
+        own = ref_hbm.at[0, :, :, lanes_of(c)]
+        line_copy(way, side, c, own, ahead).start()
+
+    def send_other(at, c):
+        way, ahead = (0, at + 1) if at == 0 else (1, at - 1)
         x_copy(c).wait_recv()
         line_copy(way, 1 - side, c, x_buf.at[c], ahead).start()
 
@@ -182,7 +175,21 @@
         def _(at=at):
             @functools.partial(loop, ends_ahead)
             def _(c):
-                send_rows(at, c)
+                send_own(at, c)
+
+    @functools.partial(loop, heads)
+    def _(c):
+        own_copy(c).start()
+
+    for a in range(3):
+        keep_copy(a).start()
+
+    for at in (0, levels - 1):
+        @pl.when(level == at)
+        def _(at=at):
+            @functools.partial(loop, ends_ahead)
+            def _(c):
+                send_other(at, c)
 
     def place(way, lev):
         return lev if way == 0 else levels - 1 - lev
@@ -260,12 +267,17 @@
         mixed += jnp.dot(w_ref.astype(jnp.bfloat16), ref_v, preferred_element_type=jnp.float32)
         return (mixed / total).astype(jnp.bfloat16)
 
-    last_lag = levels - 1
+    last_lag = levels
     units = per_dev * n_sp
     at_once = 2
-    first_unit = heads - 1 + last_lag - (per_dev - 1) * n_sp // at_once
-
-    @functools.partial(loop, max(heads + last_lag, first_unit + units // at_once))
+    per_head = n_sp // at_once
+    last_start = heads - 1 + last_lag
+    first_unit = max(
+        [3 * heads // 4]
+        + [(n + 1) * n_sp - 1 + last_lag - n * per_head for n in range(per_dev - 1)]
+    )
+
+    @functools.partial(loop, last_start + per_head)
     def _(i):
         @pl.when(i + x_ahead < heads)
         def _():
@@ -274,6 +286,10 @@
         @pl.when(jnp.logical_and(inner, i < heads))
         def _():
             x_copy(i).wait_recv()
+
+        @pl.when(i < heads)
+        def _():
+            own_copy(i).wait()
 
         for at in range(levels):
             @pl.when(level == at)
@@ -281,12 +297,13 @@
                 if at in (0, levels - 1):
                     @pl.when(i + ends_ahead < heads)
                     def _():
-                        send_rows(at, i + ends_ahead)
+                        send_own(at, i + ends_ahead)
+                        send_other(at, i + ends_ahead)
 
                 for p, way in sorted((place(way, at), way) for way in (0, 1)):
                     if p == 0:
                         continue
-                    c = i - (0 if p == 1 else p)
+                    c = i - (0 if p == 1 else p + 1)
 
                     @pl.when(jnp.logical_and(c >= 0, c < heads))
                     def _(c=c, way=way):
@@ -309,9 +326,14 @@
                     def _(a=a):
                         seq_copy(a, dest, sp).start()
 
-        unit = (i - first_unit) * at_once
-
-        @pl.when(jnp.logical_and(unit >= 0, unit < units))
+        early = (i - first_unit) * at_once
+        late = (i - last_start) * at_once + units - n_sp
+        unit = jnp.where(i >= last_start, late, early)
+        due = jnp.logical_or(
+            jnp.logical_and(early >= 0, early < units - n_sp), i >= last_start
+        )
+
+        @pl.when(due)
         def _():
             local, turn = unit // n_sp, unit % n_sp
 

time: 74.8 us -> 82.5 us (1.10)
  Pallas kernels: 72.5 us -> 80.2 us
    pallas_call x1, Pallas kernels: 72.5 us -> 80.2 us  [shards(): pl.pallas_call(functools.partial(kernel, n_grp, n_sp), out_shape=jax.Shap...]
where the time goes in v4:
time: 82.5 us; the launch traced here: 82.3 us
  Pallas kernels  80.2 us (97%)
  local copies, waits for them, and re-layouts  2.09 us (3%)
    pallas_call x1, Pallas kernels, shards(): pl.pallas_call(functools.partial(kernel, n_grp, n_sp), out_shape=jax.Shap...  80.2 us
    unnamed x1, local copies, waits for them, and re-layouts  2.09 us

profile of v4, /device:TPU:1, one launch (start us, length us, event | category | flops | bytes accessed | tf_op | source)
XLA Modules:
  0.0 82.3 jit_solution(17383990805510234541)
XLA Ops:
  0.0 80.2 %shard_map.73 = bf16[1,192,2048]{2,1,0:T(8,128)(2,1)} custom-call(s32[8]{0:T(128)} %ids_ref.1, s32[8]{0:T(128)} %owner_ref.1, s32[8]{0:T(128)} %lens_ref.1, bf16[1,192,2048]{2,1,0:T(8,128)(2,1)} %q_hbm.1, bf16[1,192,2048]{2,1,0:T(8,128)(2,1)} %k_hbm.1, bf16[1,192,2048]{2,1,0:T(8,128)(2,1)} %v_hbm.1, bf16[1,2,128,2048]{3,2,1,0:T(8,128)(2,1)} %ref_hbm.1), custom_call_target="tpu_custom_call" | custom-call | flops 2013265920 | bytes 6291456 | tf_op jit(solution)/shard_map/pallas_call | solution.py:417
  80.2 2.1 %copy.9 = bf16[1,192,2048]{2,1,0:T(8,128)(2,1)} copy(bf16[1,192,2048]{2,1,0:T(8,128)(2,1)} %shard_map.73) | data formatting | bytes 1572864

commit v5 on v4

--- a/solution.py
+++ b/solution.py
@@ -143,7 +143,7 @@
             return carry
         lax.fori_loop(0, count, step, 0)
 
-    x_ahead, ends_ahead = 10, 8
+    x_ahead, ends_ahead = 8, 6
     seq_copies = 3 * (n_sp - 1)
     per_step = -(-seq_copies // 9)
 
@@ -173,9 +173,7 @@
     for at in (0, levels - 1):
         @pl.when(level == at)
         def _(at=at):
-            @functools.partial(loop, ends_ahead)
-            def _(c):
-                send_own(at, c)
+            send_own(at, 0)
 
     @functools.partial(loop, heads)
     def _(c):
@@ -190,6 +188,7 @@
             @functools.partial(loop, ends_ahead)
             def _(c):
                 send_other(at, c)
+                send_own(at, c + 1)
 
     def place(way, lev):
         return lev if way == 0 else levels - 1 - lev
@@ -297,8 +296,11 @@
                 if at in (0, levels - 1):
                     @pl.when(i + ends_ahead < heads)
                     def _():
-                        send_own(at, i + ends_ahead)
                         send_other(at, i + ends_ahead)
+
+                    @pl.when(i + ends_ahead + 1 < heads)
+                    def _():
+                        send_own(at, i + ends_ahead + 1)
 
                 for p, way in sorted((place(way, at), way) for way in (0, 1)):
                     if p == 0:

time: 82.5 us -> 75 us (0.909)
  Pallas kernels: 80.2 us -> 72.7 us
    pallas_call x1, Pallas kernels: 80.2 us -> 72.7 us  [shards(): pl.pallas_call(functools.partial(kernel, n_grp, n_sp), out_shape=jax.Shap...]
where the time goes in v5:
time: 75 us; the launch traced here: 74.8 us
  Pallas kernels  72.7 us (97%)
  local copies, waits for them, and re-layouts  2.09 us (3%)
    pallas_call x1, Pallas kernels, shards(): pl.pallas_call(functools.partial(kernel, n_grp, n_sp), out_shape=jax.Shap...  72.7 us
    unnamed x1, local copies, waits for them, and re-layouts  2.09 us

profile of v5, /device:TPU:1, one launch (start us, length us, event | category | flops | bytes accessed | tf_op | source)
XLA Modules:
  0.0 74.8 jit_solution(4640127108253396124)
XLA Ops:
  0.0 72.7 %shard_map.73 = bf16[1,192,2048]{2,1,0:T(8,128)(2,1)} custom-call(s32[8]{0:T(128)} %ids_ref.1, s32[8]{0:T(128)} %owner_ref.1, s32[8]{0:T(128)} %lens_ref.1, bf16[1,192,2048]{2,1,0:T(8,128)(2,1)} %q_hbm.1, bf16[1,192,2048]{2,1,0:T(8,128)(2,1)} %k_hbm.1, bf16[1,192,2048]{2,1,0:T(8,128)(2,1)} %v_hbm.1, bf16[1,2,128,2048]{3,2,1,0:T(8,128)(2,1)} %ref_hbm.1), custom_call_target="tpu_custom_call" | custom-call | flops 2013265920 | bytes 6291456 | tf_op jit(solution)/shard_map/pallas_call | solution.py:419
  72.7 2.1 %copy.9 = bf16[1,192,2048]{2,1,0:T(8,128)(2,1)} copy(bf16[1,192,2048]{2,1,0:T(8,128)(2,1)} %shard_map.73) | data formatting | bytes 1572864

commit v6 on v5

--- a/solution.py
+++ b/solution.py
@@ -30,8 +30,8 @@
 def kernel(
     n_grp, n_sp,
     ids_ref, owner_ref, lens_ref, q_hbm, k_hbm, v_hbm, ref_hbm, out_hbm,
-    q_buf, k_buf, v_buf, own_buf, x_buf, line_in, line_out, routed, ref_kv, o_buf,
-    own_sem, keep_sem, seq_send, seq_recv, x_send, x_recv, line_send, line_recv,
+    q_buf, k_buf, v_buf, q_stage, k_stage, v_stage, own_buf, x_buf, line_in, line_out, routed, ref_kv, o_buf,
+    own_sem, keep_sem, stage_sem, seq_send, seq_recv, x_send, x_recv, line_send, line_recv,
     ref_send, ref_recv, o_keep, o_send, o_recv,
 ):
     levels = n_grp // PAIR
@@ -49,26 +49,6 @@
     def at_level(other):
         return (other * PAIR + side, sp)
 
-    barrier = pltpu.get_barrier_semaphore()
-
-    def greet(device):
-        pl.semaphore_signal(barrier, inc=1, device_id=device, device_id_type=MESH)
-
-    greet((mate, sp))
-    for step in range(1, n_sp):
-        greet((grp, (sp + step) % n_sp))
-
-    @pl.when(level > 0)
-    def _():
-        greet(at_level(level - 1))
-
-    @pl.when(level < levels - 1)
-    def _():
-        greet(at_level(level + 1))
-
-    inner = jnp.logical_and(level > 0, level < levels - 1)
-    pl.semaphore_wait(barrier, n_sp + 1 + inner.astype(jnp.int32))
-
     def head_of(c):
         return (c + sp) % n_sp, c // n_sp
 
@@ -83,7 +63,7 @@
 
     def x_copy(c):
         return pltpu.make_async_remote_copy(
-            src_ref=ref_hbm.at[0, :, :, lanes_of(c)], dst_ref=x_buf.at[c],
+            src_ref=own_buf.at[c], dst_ref=x_buf.at[c],
             send_sem=x_send.at[c], recv_sem=x_recv.at[c],
             device_id=(mate, sp), device_id_type=MESH,
         )
@@ -102,23 +82,31 @@
             device_id=(grp, dest), device_id_type=MESH,
         )
 
-    seq_pairs = ((q_hbm, q_buf), (k_hbm, k_buf), (v_hbm, v_buf))
+    seq_refs = (
+        (q_hbm, q_stage, q_buf), (k_hbm, k_stage, k_buf), (v_hbm, v_stage, v_buf)
+    )
 
     def seq_lanes(dest):
         return pl.ds(pl.multiple_of(dest * feat, HEAD_DIM), feat)
 
     def seq_copy(a, dest, src):
-        hbm, buf = seq_pairs[a]
+        _, stage, buf = seq_refs[a]
         return pltpu.make_async_remote_copy(
-            src_ref=hbm.at[0, :, seq_lanes(dest)], dst_ref=buf.at[src],
+            src_ref=stage.at[dest], dst_ref=buf.at[src],
             send_sem=seq_send.at[a, dest], recv_sem=seq_recv.at[a, src],
             device_id=(grp, dest), device_id_type=MESH,
         )
 
     def keep_copy(a):
-        hbm, buf = seq_pairs[a]
+        hbm, _, buf = seq_refs[a]
         return pltpu.make_async_copy(
             hbm.at[0, :, seq_lanes(sp)], buf.at[sp], keep_sem.at[a]
+        )
+
+    def stage_copy(a, dest):
+        hbm, stage, _ = seq_refs[a]
+        return pltpu.make_async_copy(
+            hbm.at[0, :, seq_lanes(dest)], stage.at[dest], stage_sem.at[a, dest]
         )
 
     def o_copy(local, dest, src):
@@ -147,6 +135,43 @@
     seq_copies = 3 * (n_sp - 1)
     per_step = -(-seq_copies // 9)
 
+    inner = jnp.logical_and(level > 0, level < levels - 1)
+
+    @functools.partial(loop, heads)
+    def _(c):
+        own_copy(c).start()
+
+    @functools.partial(loop, n_sp - 1)
+    def _(step):
+        for a in range(3):
+            stage_copy(a, (sp + 1 + step) % n_sp).start()
+
+    for a in range(3):
+        keep_copy(a).start()
+
+    barrier = pltpu.get_barrier_semaphore()
+
+    def greet(device):
+        pl.semaphore_signal(barrier, inc=1, device_id=device, device_id_type=MESH)
+
+    greet((mate, sp))
+    for step in range(1, n_sp):
+        greet((grp, (sp + step) % n_sp))
+
+    @pl.when(level > 0)
+    def _():
+        greet(at_level(level - 1))
+
+    @pl.when(level < levels - 1)
+    def _():
+        greet(at_level(level + 1))
+
+    pl.semaphore_wait(barrier, n_sp + 1 + inner.astype(jnp.int32))
+
+    @functools.partial(loop, heads)
+    def _(c):
+        own_copy(c).wait()
+
     @functools.partial(loop, x_ahead)
     def _(c):
         x_copy(c).start()
@@ -162,8 +187,7 @@
 
     def send_own(at, c):
         way, ahead = (0, at + 1) if at == 0 else (1, at - 1)
-        own = ref_hbm.at[0, :, :, lanes_of(c)]
-        line_copy(way, side, c, own, ahead).start()
+        line_copy(way, side, c, own_buf.at[c], ahead).start()
 
     def send_other(at, c):
         way, ahead = (0, at + 1) if at == 0 else (1, at - 1)
@@ -175,16 +199,6 @@
         def _(at=at):
             send_own(at, 0)
 
-    @functools.partial(loop, heads)
-    def _(c):
-        own_copy(c).start()
-
-    for a in range(3):
-        keep_copy(a).start()
-
-    for at in (0, levels - 1):
-        @pl.when(level == at)
-        def _(at=at):
             @functools.partial(loop, ends_ahead)
             def _(c):
                 send_other(at, c)
@@ -286,10 +300,6 @@
         def _():
             x_copy(i).wait_recv()
 
-        @pl.when(i < heads)
-        def _():
-            own_copy(i).wait()
-
         for at in range(levels):
             @pl.when(level == at)
             def _(at=at):
@@ -326,6 +336,7 @@
                 for a in range(3):
                     @pl.when(number % 3 == a)
                     def _(a=a):
+                        stage_copy(a, dest).wait()
                         seq_copy(a, dest, sp).start()
 
         early = (i - first_unit) * at_once
@@ -425,6 +436,9 @@
             pltpu.VMEM((n_sp, tokens, feat), bf16),
             pltpu.VMEM((n_sp, tokens, feat), bf16),
             pltpu.VMEM((n_sp, tokens, feat), bf16),
+            pltpu.VMEM((n_sp, tokens, feat), bf16),
+            pltpu.VMEM((n_sp, tokens, feat), bf16),
+            pltpu.VMEM((n_sp, tokens, feat), bf16),
             pltpu.VMEM((heads,) + chunk, bf16),
             pltpu.VMEM((heads,) + chunk, bf16),
             pltpu.VMEM((2, slots, heads) + chunk, bf16),
@@ -434,6 +448,7 @@
             pltpu.VMEM((n_sp, tokens, feat), bf16),
             dma((heads,)),
             dma((3,)),
+            dma((3, n_sp)),
             dma((3, n_sp)),
             dma((3, n_sp)),
             dma((heads,)),

time: 75 us -> 75.3 us (level)
  no operation moved by 1% of the time
where the time goes in v6:
time: 75.3 us; the launch traced here: 75.1 us
  Pallas kernels  73 us (97%)
  local copies, waits for them, and re-layouts  2.09 us (3%)
    pallas_call x1, Pallas kernels, shards(): pl.pallas_call(functools.partial(kernel, n_grp, n_sp), out_shape=jax.Shap...  73 us
    unnamed x1, local copies, waits for them, and re-layouts  2.09 us

profile of v6, /device:TPU:1, one launch (start us, length us, event | category | flops | bytes accessed | tf_op | source)
XLA Modules:
  0.0 75.1 jit_solution(751959892988499140)
XLA Ops:
  0.0 73.0 %shard_map.73 = bf16[1,192,2048]{2,1,0:T(8,128)(2,1)} custom-call(s32[8]{0:T(128)} %ids_ref.1, s32[8]{0:T(128)} %owner_ref.1, s32[8]{0:T(128)} %lens_ref.1, bf16[1,192,2048]{2,1,0:T(8,128)(2,1)} %q_hbm.1, bf16[1,192,2048]{2,1,0:T(8,128)(2,1)} %k_hbm.1, bf16[1,192,2048]{2,1,0:T(8,128)(2,1)} %v_hbm.1, bf16[1,2,128,2048]{3,2,1,0:T(8,128)(2,1)} %ref_hbm.1), custom_call_target="tpu_custom_call" | custom-call | flops 2013265920 | bytes 6291456 | tf_op jit(solution)/shard_map/pallas_call | solution.py:430
  73.0 2.1 %copy.9 = bf16[1,192,2048]{2,1,0:T(8,128)(2,1)} copy(bf16[1,192,2048]{2,1,0:T(8,128)(2,1)} %shard_map.73) | data formatting | bytes 1572864

commit v7 on v6

--- a/solution.py
+++ b/solution.py
@@ -49,8 +49,13 @@
     def at_level(other):
         return (other * PAIR + side, sp)
 
+    chunks = 2 * heads
+
     def head_of(c):
-        return (c + sp) % n_sp, c // n_sp
+        return (c // 2 + sp) % n_sp, c // (2 * n_sp)
+
+    def turn_of(step):
+        return (sp // 2 * 2 + 2 + step) % n_sp
 
     def lanes_of(c):
         dest, local = head_of(c)
@@ -58,7 +63,7 @@
 
     def own_copy(c):
         return pltpu.make_async_copy(
-            ref_hbm.at[0, :, :, lanes_of(c)], own_buf.at[c], own_sem.at[c]
+            ref_hbm.at[0, c % 2, :, lanes_of(c)], own_buf.at[c], own_sem.at[c]
         )
 
     def x_copy(c):
@@ -76,9 +81,10 @@
         )
 
     def ref_copy(c, dest, local, src):
+        half = c % 2
         return pltpu.make_async_remote_copy(
-            src_ref=routed.at[c], dst_ref=ref_kv.at[local, src],
-            send_sem=ref_send.at[c], recv_sem=ref_recv.at[local, src],
+            src_ref=routed.at[c], dst_ref=ref_kv.at[local, half, src],
+            send_sem=ref_send.at[c], recv_sem=ref_recv.at[local, half, src],
             device_id=(grp, dest), device_id_type=MESH,
         )
 
@@ -131,13 +137,13 @@
             return carry
         lax.fori_loop(0, count, step, 0)
 
-    x_ahead, ends_ahead = 8, 6
-    seq_copies = 3 * (n_sp - 1)
-    per_step = -(-seq_copies // 9)
+    x_ahead, ends_ahead = 13, 10
+    seq_copies = 3 * n_sp
+    per_step = -(-seq_copies // 12)
 
     inner = jnp.logical_and(level > 0, level < levels - 1)
 
-    @functools.partial(loop, heads)
+    @functools.partial(loop, chunks)
     def _(c):
         own_copy(c).start()
 
@@ -168,7 +174,7 @@
 
     pl.semaphore_wait(barrier, n_sp + 1 + inner.astype(jnp.int32))
 
-    @functools.partial(loop, heads)
+    @functools.partial(loop, chunks)
     def _(c):
         own_copy(c).wait()
 
@@ -249,7 +255,7 @@
 
         @pl.when(dest == sp)
         def _():
-            ref_kv[local, sp] = value
+            ref_kv[local, c % 2, sp] = value
 
         @pl.when(dest != sp)
         def _():
@@ -262,8 +268,8 @@
         q = q_buf[block, :, lanes]
         k = k_buf[:, :, lanes].reshape(own_keys, HEAD_DIM)
         v = v_buf[:, :, lanes].reshape(own_keys, HEAD_DIM)
-        ref_k = ref_kv[local, :, 0].reshape(ref_keys, HEAD_DIM)
-        ref_v = ref_kv[local, :, 1].reshape(ref_keys, HEAD_DIM)
+        ref_k = ref_kv[local, 0].reshape(ref_keys, HEAD_DIM)
+        ref_v = ref_kv[local, 1].reshape(ref_keys, HEAD_DIM)
         contract = (((1,), (1,)), ((), ()))
         scale = HEAD_DIM ** -0.5
         s_own = lax.dot_general(q, k, contract, preferred_element_type=jnp.float32) * scale
@@ -280,23 +286,23 @@
         mixed += jnp.dot(w_ref.astype(jnp.bfloat16), ref_v, preferred_element_type=jnp.float32)
         return (mixed / total).astype(jnp.bfloat16)
 
-    last_lag = levels
+    last_lag = 2 * (levels - 1)
     units = per_dev * n_sp
     at_once = 2
     per_head = n_sp // at_once
-    last_start = heads - 1 + last_lag
+    last_start = chunks - 1 + last_lag
     first_unit = max(
-        [3 * heads // 4]
-        + [(n + 1) * n_sp - 1 + last_lag - n * per_head for n in range(per_dev - 1)]
+        [3 * chunks // 4]
+        + [2 * (n + 1) * n_sp - 1 + last_lag - 2 * n * per_head for n in range(per_dev - 1)]
     )
 
     @functools.partial(loop, last_start + per_head)
     def _(i):
-        @pl.when(i + x_ahead < heads)
+        @pl.when(i + x_ahead < chunks)
         def _():
             x_copy(i + x_ahead).start()
 
-        @pl.when(jnp.logical_and(inner, i < heads))
+        @pl.when(jnp.logical_and(inner, i < chunks))
         def _():
             x_copy(i).wait_recv()
 
@@ -304,46 +310,51 @@
             @pl.when(level == at)
             def _(at=at):
                 if at in (0, levels - 1):
-                    @pl.when(i + ends_ahead < heads)
+                    @pl.when(i + ends_ahead < chunks)
                     def _():
                         send_other(at, i + ends_ahead)
 
-                    @pl.when(i + ends_ahead + 1 < heads)
+                    @pl.when(i + ends_ahead + 1 < chunks)
                     def _():
                         send_own(at, i + ends_ahead + 1)
 
                 for p, way in sorted((place(way, at), way) for way in (0, 1)):
                     if p == 0:
                         continue
-                    c = i - (0 if p == 1 else p + 1)
-
-                    @pl.when(jnp.logical_and(c >= 0, c < heads))
+                    c = i - (0 if p == 1 else 2 * p)
+
+                    @pl.when(jnp.logical_and(c >= 0, c < chunks))
                     def _(c=c, way=way):
                         relay(at, way, c)
 
                 done = i - last_lag
 
-                @pl.when(jnp.logical_and(done >= 0, done < heads))
+                @pl.when(jnp.logical_and(done >= 0, done < chunks))
                 def _():
                     final(at, done)
 
         for n in range(per_step):
-            number = i * per_step + n
-
-            @pl.when(number < seq_copies)
-            def _(number=number):
-                dest = (sp + 1 + number // 3) % n_sp
+            number = i // 2 * per_step + n
+            dest = turn_of(number // 3)
+            start = jnp.logical_and(i % 2 == 0, number < seq_copies)
+
+            @pl.when(jnp.logical_and(start, dest != sp))
+            def _(number=number, dest=dest):
                 for a in range(3):
                     @pl.when(number % 3 == a)
                     def _(a=a):
                         stage_copy(a, dest).wait()
                         seq_copy(a, dest, sp).start()
 
-        early = (i - first_unit) * at_once
+        early = (i - first_unit) // 2 * at_once
         late = (i - last_start) * at_once + units - n_sp
         unit = jnp.where(i >= last_start, late, early)
         due = jnp.logical_or(
-            jnp.logical_and(early >= 0, early < units - n_sp), i >= last_start
+            jnp.logical_and(
+                jnp.logical_and(i >= first_unit, (i - first_unit) % 2 == 0),
+                early < units - n_sp,
+            ),
+            i >= last_start,
         )
 
         @pl.when(due)
@@ -367,9 +378,10 @@
                 def _(step):
                     src = (sp + 1 + step) % n_sp
                     ref_copy(0, sp, local, src).wait_recv()
+                    ref_copy(1, sp, local, src).wait_recv()
 
             lanes = pl.ds(pl.multiple_of(local * HEAD_DIM, HEAD_DIM), HEAD_DIM)
-            blocks = [(sp + 1 + turn + n) % n_sp for n in range(at_once)]
+            blocks = [turn_of(turn + n) for n in range(at_once)]
             results = [attend(local, block) for block in blocks]
             for block, result in zip(blocks, results):
                 o_buf[block, :, lanes] = result
@@ -382,7 +394,7 @@
                 def _(block=block):
                     o_copy(local, block, sp).start()
 
-    @functools.partial(loop, heads)
+    @functools.partial(loop, chunks)
     def _(c):
         x_copy(c).wait_send()
         dest, local = head_of(c)
@@ -417,11 +429,12 @@
     tokens, width = queries.shape[1:]
     ref_tokens = ref_cache.shape[2]
     heads = width // HEAD_DIM
+    chunks = 2 * heads
     per_dev = heads // n_sp
     feat = per_dev * HEAD_DIM
     levels = n_grp // PAIR
     slots = max(slots_on(p, levels) for p in range(levels - 1))
-    chunk = (2, ref_tokens, HEAD_DIM)
+    chunk = (ref_tokens, HEAD_DIM)
     bf16 = jnp.bfloat16
     dma = pltpu.SemaphoreType.DMA
     smem = pl.BlockSpec(memory_space=pltpu.SMEM)
@@ -439,24 +452,24 @@
             pltpu.VMEM((n_sp, tokens, feat), bf16),
             pltpu.VMEM((n_sp, tokens, feat), bf16),
             pltpu.VMEM((n_sp, tokens, feat), bf16),
-            pltpu.VMEM((heads,) + chunk, bf16),
-            pltpu.VMEM((heads,) + chunk, bf16),
-            pltpu.VMEM((2, slots, heads) + chunk, bf16),
-            pltpu.VMEM((2, slots, heads) + chunk, bf16),
-            pltpu.VMEM((heads,) + chunk, bf16),
-            pltpu.VMEM((per_dev, n_sp) + chunk, bf16),
-            pltpu.VMEM((n_sp, tokens, feat), bf16),
-            dma((heads,)),
+            pltpu.VMEM((chunks,) + chunk, bf16),
+            pltpu.VMEM((chunks,) + chunk, bf16),
+            pltpu.VMEM((2, slots, chunks) + chunk, bf16),
+            pltpu.VMEM((2, slots, chunks) + chunk, bf16),
+            pltpu.VMEM((chunks,) + chunk, bf16),
+            pltpu.VMEM((per_dev, 2, n_sp) + chunk, bf16),
+            pltpu.VMEM((n_sp, tokens, feat), bf16),
+            dma((chunks,)),
             dma((3,)),
             dma((3, n_sp)),
             dma((3, n_sp)),
             dma((3, n_sp)),
-            dma((heads,)),
-            dma((heads,)),
-            dma((2, slots, heads)),
-            dma((2, slots, heads)),
-            dma((heads,)),
-            dma((per_dev, n_sp)),
+            dma((chunks,)),
+            dma((chunks,)),
+            dma((2, slots, chunks)),
+            dma((2, slots, chunks)),
+            dma((chunks,)),
+            dma((per_dev, 2, n_sp)),
             dma((per_dev,)),
             dma((per_dev, n_sp)),
             dma((per_dev, n_sp)),

time: 75.3 us -> 76.3 us (1.013)
  Pallas kernels: 73 us -> 74 us
    pallas_call x1, Pallas kernels: 73 us -> 74 us  [shards(): pl.pallas_call(functools.partial(kernel, n_grp, n_sp), out_shape=jax.Shap...]
where the time goes in v7:
time: 76.3 us; the launch traced here: 76.1 us
  Pallas kernels  74 us (97%)
  local copies, waits for them, and re-layouts  2.09 us (3%)
    pallas_call x1, Pallas kernels, shards(): pl.pallas_call(functools.partial(kernel, n_grp, n_sp), out_shape=jax.Shap...  74 us
    unnamed x1, local copies, waits for them, and re-layouts  2.09 us

profile of v7, /device:TPU:1, one launch (start us, length us, event | category | flops | bytes accessed | tf_op | source)
XLA Modules:
  0.0 76.1 jit_solution(17653887443377861972)
XLA Ops:
  0.0 74.0 %shard_map.73 = bf16[1,192,2048]{2,1,0:T(8,128)(2,1)} custom-call(s32[8]{0:T(128)} %ids_ref.1, s32[8]{0:T(128)} %owner_ref.1, s32[8]{0:T(128)} %lens_ref.1, bf16[1,192,2048]{2,1,0:T(8,128)(2,1)} %q_hbm.1, bf16[1,192,2048]{2,1,0:T(8,128)(2,1)} %k_hbm.1, bf16[1,192,2048]{2,1,0:T(8,128)(2,1)} %v_hbm.1, bf16[1,2,128,2048]{3,2,1,0:T(8,128)(2,1)} %ref_hbm.1), custom_call_target="tpu_custom_call" | custom-call | flops 2013265920 | bytes 6291456 | tf_op jit(solution)/shard_map/pallas_call | solution.py:443
  74.0 2.1 %copy.9 = bf16[1,192,2048]{2,1,0:T(8,128)(2,1)} copy(bf16[1,192,2048]{2,1,0:T(8,128)(2,1)} %shard_map.73) | data formatting | bytes 1572864

commit v8 on v6

--- a/solution.py
+++ b/solution.py
@@ -1,4 +1,5 @@
 import functools
+import math
 
 import jax
 import jax.numpy as jnp
@@ -55,6 +56,9 @@
     def lanes_of(c):
         dest, local = head_of(c)
         return pl.ds(pl.multiple_of((dest * per_dev + local) * HEAD_DIM, HEAD_DIM), HEAD_DIM)
+
+    def turn_of(step):
+        return (sp // 2 * 2 + 2 + step) % n_sp
 
     def own_copy(c):
         return pltpu.make_async_copy(
@@ -265,16 +269,16 @@
         ref_k = ref_kv[local, :, 0].reshape(ref_keys, HEAD_DIM)
         ref_v = ref_kv[local, :, 1].reshape(ref_keys, HEAD_DIM)
         contract = (((1,), (1,)), ((), ()))
-        scale = HEAD_DIM ** -0.5
-        s_own = lax.dot_general(q, k, contract, preferred_element_type=jnp.float32) * scale
-        s_ref = lax.dot_general(q, ref_k, contract, preferred_element_type=jnp.float32) * scale
+        scale = HEAD_DIM ** -0.5 * math.log2(math.e)
+        s_own = lax.dot_general(q, k, contract, preferred_element_type=jnp.float32)
+        s_ref = lax.dot_general(q, ref_k, contract, preferred_element_type=jnp.float32)
         col = lax.broadcasted_iota(jnp.int32, s_ref.shape, 1)
         s_ref = jnp.where(col < live, s_ref, -jnp.inf)
         peak = jnp.maximum(
             jnp.max(s_own, axis=1, keepdims=True), jnp.max(s_ref, axis=1, keepdims=True)
         )
-        w_own = jnp.exp(s_own - peak)
-        w_ref = jnp.exp(s_ref - peak)
+        w_own = jnp.exp2((s_own - peak) * scale)
+        w_ref = jnp.exp2((s_ref - peak) * scale)
         total = jnp.sum(w_own, axis=1, keepdims=True) + jnp.sum(w_ref, axis=1, keepdims=True)
         mixed = jnp.dot(w_own.astype(jnp.bfloat16), v, preferred_element_type=jnp.float32)
         mixed += jnp.dot(w_ref.astype(jnp.bfloat16), ref_v, preferred_element_type=jnp.float32)
@@ -369,7 +373,7 @@
                     ref_copy(0, sp, local, src).wait_recv()
 
             lanes = pl.ds(pl.multiple_of(local * HEAD_DIM, HEAD_DIM), HEAD_DIM)
-            blocks = [(sp + 1 + turn + n) % n_sp for n in range(at_once)]
+            blocks = [turn_of(turn + n) for n in range(at_once)]
             results = [attend(local, block) for block in blocks]
             for block, result in zip(blocks, results):
                 o_buf[block, :, lanes] = result

time: 75.3 us -> 74.9 us (level)
  no operation moved by 1% of the time
where the time goes in v8:
time: 74.9 us; the launch traced here: 74.8 us
  Pallas kernels  72.7 us (97%)
  local copies, waits for them, and re-layouts  2.09 us (3%)
    pallas_call x1, Pallas kernels, shards(): pl.pallas_call(functools.partial(kernel, n_grp, n_sp), out_shape=jax.Shap...  72.7 us
    unnamed x1, local copies, waits for them, and re-layouts  2.09 us

profile of v8, /device:TPU:1, one launch (start us, length us, event | category | flops | bytes accessed | tf_op | source)
XLA Modules:
  0.0 74.8 jit_solution(6284238879246714057)
XLA Ops:
  0.0 72.7 %shard_map.73 = bf16[1,192,2048]{2,1,0:T(8,128)(2,1)} custom-call(s32[8]{0:T(128)} %ids_ref.1, s32[8]{0:T(128)} %owner_ref.1, s32[8]{0:T(128)} %lens_ref.1, bf16[1,192,2048]{2,1,0:T(8,128)(2,1)} %q_hbm.1, bf16[1,192,2048]{2,1,0:T(8,128)(2,1)} %k_hbm.1, bf16[1,192,2048]{2,1,0:T(8,128)(2,1)} %v_hbm.1, bf16[1,2,128,2048]{3,2,1,0:T(8,128)(2,1)} %ref_hbm.1), custom_call_target="tpu_custom_call" | custom-call | flops 2013265920 | bytes 6291456 | tf_op jit(solution)/shard_map/pallas_call | solution.py:434
  72.7 2.1 %copy.9 = bf16[1,192,2048]{2,1,0:T(8,128)(2,1)} copy(bf16[1,192,2048]{2,1,0:T(8,128)(2,1)} %shard_map.73) | data formatting | bytes 1572864

commit v9 on v8

--- a/solution.py
+++ b/solution.py
@@ -417,6 +417,21 @@
         o_here(local).wait()
 
 
+def hand_over(src, dst, sems):
+    pieces = sems.shape[0]
+    rows = src.shape[1] // pieces
+    copies = [
+        pltpu.make_async_copy(
+            src.at[:, n * rows:(n + 1) * rows], dst.at[:, n * rows:(n + 1) * rows], sems.at[n]
+        )
+        for n in range(pieces)
+    ]
+    for copy in copies:
+        copy.start()
+    for copy in copies:
+        copy.wait()
+
+
 def shards(n_grp, n_sp, queries, keys, values, ref_cache, ref_ids, ref_owner, ref_lens):
     tokens, width = queries.shape[1:]
     ref_tokens = ref_cache.shape[2]
@@ -431,7 +446,7 @@
     smem = pl.BlockSpec(memory_space=pltpu.SMEM)
     hbm = pl.BlockSpec(memory_space=pl.ANY)
     all_keys = n_sp * (tokens + ref_tokens)
-    return pl.pallas_call(
+    attended = pl.pallas_call(
         functools.partial(kernel, n_grp, n_sp),
         out_shape=jax.ShapeDtypeStruct(queries.shape, bf16),
         in_specs=[smem] * 3 + [hbm] * 4,
@@ -474,6 +489,13 @@
             transcendentals=per_dev * n_sp * tokens * all_keys,
         ),
     )(ref_ids, ref_owner, ref_lens, queries, keys, values, ref_cache)
+    return pl.pallas_call(
+        hand_over,
+        out_shape=jax.ShapeDtypeStruct(queries.shape, bf16),
+        in_specs=[hbm],
+        out_specs=hbm,
+        scratch_shapes=[dma((4,))],
+    )(attended)
 
 
 def solution(mesh):

time: 74.9 us -> 97.8 us (1.31)
  Pallas kernels: 72.7 us -> 97.7 us
  local copies, waits for them, and re-layouts: 2.09 us -> 0 us
    pallas_call x0 -> x1, Pallas kernels: none -> 25 us  [shards(): pl.pallas_call(hand_over, out_shape=jax.ShapeDtypeStruct(queries.shape, b...]
    unnamed x1 -> x0, local copies, waits for them, and re-layouts: 2.09 us -> none
where the time goes in v9:
time: 97.8 us; the launch traced here: 97.7 us
  Pallas kernels  97.7 us (100%)
    pallas_call x1, Pallas kernels, shards(): pl.pallas_call(functools.partial(kernel, n_grp, n_sp), out_shape=jax.Shap...  72.7 us
    pallas_call x1, Pallas kernels, shards(): pl.pallas_call(hand_over, out_shape=jax.ShapeDtypeStruct(queries.shape, b...  25 us

profile of v9, /device:TPU:1, one launch (start us, length us, event | category | flops | bytes accessed | tf_op | source)
XLA Modules:
  0.0 97.7 jit_solution(5958262085178085762)
XLA Ops:
  0.0 72.7 %shard_map.73.src = bf16[1,192,2048]{2,1,0:T(8,128)(2,1)} custom-call(s32[8]{0:T(128)} %ids_ref.1, s32[8]{0:T(128)} %owner_ref.1, s32[8]{0:T(128)} %lens_ref.1, bf16[1,192,2048]{2,1,0:T(8,128)(2,1)} %q_hbm.1, bf16[1,192,2048]{2,1,0:T(8,128)(2,1)} %k_hbm.1, bf16[1,192,2048]{2,1,0:T(8,128)(2,1)} %v_hbm.1, bf16[1,2,128,2048]{3,2,1,0:T(8,128)(2,1)} %ref_hbm.1), custom_call_target="tpu_custom_call" | custom-call | flops 2013265920 | bytes 6291456 | tf_op jit(solution)/shard_map/pallas_call | solution.py:449
  72.7 25.0 %shard_map.74 = bf16[1,192,2048]{2,1,0:T(8,128)(2,1)} custom-call(bf16[1,192,2048]{2,1,0:T(8,128)(2,1)} %shard_map.73.src), custom_call_target="tpu_custom_call" | custom-call | tf_op jit(solution)/shard_map/pallas_call | solution.py:492
